TPU v7x, 256 devices: a whole 4x4x8 slice. The times are simulated.
256 devices in a mesh: section: 8 (over z_lo, x), seq: 32 (over z_hi, y, core).
Axes of the slice: x: 4, y: 4, z: 8 (z_hi: 4, z_lo: 2; z = z_hi * 2 + z_lo), core: 2. Of those that a mesh axis runs over, the one named last changes fastest.
Arguments:
- queries: bfloat16 [8, 3072, 4096], P('section', 'seq'), may hold values from -120 to 120
- keys: bfloat16 [8, 3072, 4096], P('section', 'seq'), may hold values from -120 to 120
- values: bfloat16 [8, 3072, 4096], P('section', 'seq'), may hold values from -6 to 6
- norm_gains: float32 [2, 4096], replicated, may hold values from 1.2 to 2.5
Outputs:
- attended: bfloat16 [8, 3072, 4096], P('section', 'seq')
All inputs are finite; a program needn't handle non-finite values.
Results may differ from a plain program's by a relative error of at most 0.0014.
The roundings to bfloat16 on the way count: a program that leaves them out, or rounds other values in their place, can miss the bound.
Values may be sent and summed in bfloat16 or wider, within the bound.
No kernel may reach another device: no remote copies, remote signals or barrier semaphores. Data moves between devices by JAX's collectives and lax.ppermute only.
A program may use at most 128 MiB of HBM per device.

v0:
```python
import math

import jax
import jax.numpy as jnp
from jax import lax
from jax.sharding import PartitionSpec as P

HEAD_DIM = 128


def passed_along(block, axis, distance):
    devices = range(lax.axis_size(axis))
    route = [(i - distance, i) for i in devices if i - distance in devices]
    return lax.ppermute(block, axis, route)


def normalize(rows, gain):
    wide = rows.astype(jnp.float32)
    power = jnp.mean(wide * wide, axis=-1, keepdims=True)
    return (wide * lax.rsqrt(power + 1e-06) * gain).astype(jnp.bfloat16)


def block_scores(query_block, key_rows):
    raw = jnp.einsum("qhd,khd->hqk", query_block, key_rows, preferred_element_type=jnp.float32)
    return raw * (1.0 / math.sqrt(HEAD_DIM))


def finish(own_scores, prior_scores, own_values, prior_values):
    top = jnp.maximum(
        jnp.max(own_scores, axis=2, keepdims=True), jnp.max(prior_scores, axis=2, keepdims=True)
    )
    own_expo = jnp.exp(own_scores - top)
    prior_expo = jnp.exp(prior_scores - top)
    total = jnp.sum(own_expo, axis=2, keepdims=True) + jnp.sum(prior_expo, axis=2, keepdims=True)
    mixed = jnp.einsum(
        "hqk,khd->qhd",
        own_expo.astype(jnp.bfloat16),
        own_values,
        preferred_element_type=jnp.float32,
    )
    mixed = mixed + jnp.einsum(
        "hqk,khd->qhd",
        prior_expo.astype(jnp.bfloat16),
        prior_values,
        preferred_element_type=jnp.float32,
    )
    return (mixed / jnp.transpose(total, (1, 0, 2))).astype(jnp.bfloat16)


def local(queries, keys, values, norm_gains):
    query_norm = normalize(queries[0], norm_gains[0])
    key_norm = normalize(keys[0], norm_gains[1])
    value_rows = values[0]
    head_queries, head_keys, head_values = (
        lax.all_to_all(query_norm, "seq", split_axis=1, concat_axis=0, tiled=True),
        lax.all_to_all(key_norm, "seq", split_axis=1, concat_axis=0, tiled=True),
        lax.all_to_all(value_rows, "seq", split_axis=1, concat_axis=0, tiled=True),
    )
    prior_keys, prior_values = passed_along((head_keys, head_values), "section", 1)
    length = head_queries.shape[0]
    head_width = head_queries.shape[1]
    heads_here = head_width // HEAD_DIM
    own_keys = head_keys.reshape(length, heads_here, HEAD_DIM)
    own_values = head_values.reshape(length, heads_here, HEAD_DIM)
    prior_keys = prior_keys.reshape(length, heads_here, HEAD_DIM)
    prior_values = prior_values.reshape(length, heads_here, HEAD_DIM)
    has_prior = lax.axis_index("section") > 0
    rows_block = min(length, 512)
    blocks = length // rows_block
    query_blocks = head_queries.reshape(blocks, rows_block, heads_here, HEAD_DIM)

    def earlier_scores(query_block):
        return jnp.where(has_prior, block_scores(query_block, prior_keys), -jnp.inf)

    def complete_joint(query_block):
        return finish(
            block_scores(query_block, own_keys),
            earlier_scores(query_block),
            own_values,
            prior_values,
        )

    mixed = lax.map(complete_joint, query_blocks)
    attended = mixed.reshape(length, head_width)
    returned = lax.all_to_all(attended, "seq", split_axis=0, concat_axis=1, tiled=True)
    return returned[None]


def solution(mesh):
    return jax.shard_map(
        local,
        mesh=mesh,
        in_specs=(
            P("section", "seq", None),
            P("section", "seq", None),
            P("section", "seq", None),
            P(),
        ),
        out_specs=P("section", "seq", None),
        check_vma=False,
    )
```

profile of v0, /device:TPU:32, one launch (start us, length us, event | category | flops | bytes accessed | tf_op | source)
XLA Modules:
  0.0 211.9 jit_solution(3551049194743910896)
XLA Ops:
  0.0 1.3 convert_bitcast_fusion
  1.3 1.4 fusion.46
  4.2 1.2 copy.28
  5.4 10.6 %all-to-all-start.1 = ((bf16[96,32,128]{2,0,1:T(8,128)(2,1)}), bf16[96,32,128]{2,0,1:T(8,128)(2,1)S(1)}, u32[]{:S(2)}, u32[]{:S(2)}) async-start(bf16[96,32,128]{2,0,1:T(8,128)(2,1)} %copy.28), calls=%async_computation.1 | async-start | bytes 1572864 | tf_op jit(solution)/shard_map/all_to_all | solution.py:56
  16.1 1.2 copy.29
  17.3 22.0 %all-to-all-done.1 = bf16[96,32,128]{2,0,1:T(8,128)(2,1)S(1)} async-done(((bf16[96,32,128]{2,0,1:T(8,128)(2,1)}), bf16[96,32,128]{2,0,1:T(8,128)(2,1)S(1)}, u32[]{:S(2)}, u32[]{:S(2)}) %all-to-all-start.1) | async-done | bytes 786464 | tf_op jit(solution)/shard_map/all_to_all | solution.py:56
  39.3 4.6 %all-to-all-start.2 = ((bf16[96,32,128]{2,0,1:T(8,128)(2,1)}), bf16[96,32,128]{2,0,1:T(8,128)(2,1)S(1)}, u32[]{:S(2)}, u32[]{:S(2)}) async-start(bf16[96,32,128]{2,0,1:T(8,128)(2,1)} %copy.29), calls=%async_computation.2 | async-start | bytes 1572864 | tf_op jit(solution)/shard_map/all_to_all | solution.py:57
  44.8 1.2 copy.27
  46.0 16.9 %all-to-all-done.2 = bf16[96,32,128]{2,0,1:T(8,128)(2,1)S(1)} async-done(((bf16[96,32,128]{2,0,1:T(8,128)(2,1)}), bf16[96,32,128]{2,0,1:T(8,128)(2,1)S(1)}, u32[]{:S(2)}, u32[]{:S(2)}) %all-to-all-start.2) | async-done | bytes 786464 | tf_op jit(solution)/shard_map/all_to_all | solution.py:57
  62.9 9.3 %all-to-all-start = ((bf16[96,32,128]{2,0,1:T(8,128)(2,1)}), bf16[96,32,128]{2,0,1:T(8,128)(2,1)S(1)}, u32[]{:S(2)}, u32[]{:S(2)}) async-start(bf16[96,32,128]{2,0,1:T(8,128)(2,1)} %copy.27), calls=%async_computation | async-start | bytes 1572864 | tf_op jit(solution)/shard_map/all_to_all | solution.py:55
  72.2 3.4 %collective-permute-start = (bf16[3072,128]{1,0:T(8,128)(2,1)S(1)}, bf16[3072,128]{1,0:T(8,128)(2,1)S(1)}, u32[]{:S(2)}, u32[]{:S(2)}) collective-permute-start(bf16[3072,128]{1,0:T(8,128)(2,1)S(1)} %bitcast.101), channel_id=1, source_target_pairs={{0,32},{32,64},{64,96},{96,128},{128,160},{160,192},{192,224},{1,3... | collective-permute-start | bytes 2359304 | tf_op jit(solution)/shard_map/ppermute | solution.py:14
  75.6 3.4 %collective-permute-start.1 = (bf16[3072,128]{1,0:T(8,128)(2,1)S(1)}, bf16[3072,128]{1,0:T(8,128)(2,1)}, u32[]{:S(2)}, u32[]{:S(2)}) collective-permute-start(bf16[3072,128]{1,0:T(8,128)(2,1)S(1)} %bitcast.103), channel_id=1, source_target_pairs={{0,32},{32,64},{64,96},{96,128},{128,160},{160,192},{192,224},{1,3... | collective-permute-start | bytes 2359304 | tf_op jit(solution)/shard_map/ppermute | solution.py:14
  79.0 12.2 %all-to-all-done = bf16[96,32,128]{2,0,1:T(8,128)(2,1)S(1)} async-done(((bf16[96,32,128]{2,0,1:T(8,128)(2,1)}), bf16[96,32,128]{2,0,1:T(8,128)(2,1)S(1)}, u32[]{:S(2)}, u32[]{:S(2)}) %all-to-all-start) | async-done | bytes 786464 | tf_op jit(solution)/shard_map/all_to_all | solution.py:55
  91.2 20.4 %collective-permute-done = bf16[3072,128]{1,0:T(8,128)(2,1)S(1)} collective-permute-done((bf16[3072,128]{1,0:T(8,128)(2,1)S(1)}, bf16[3072,128]{1,0:T(8,128)(2,1)S(1)}, u32[]{:S(2)}, u32[]{:S(2)}) %collective-permute-start) | collective-permute-done | bytes 786464 | tf_op jit(solution)/shard_map/ppermute | solution.py:14
  111.6 16.7 %collective-permute-done.1 = bf16[3072,128]{1,0:T(8,128)(2,1)} collective-permute-done((bf16[3072,128]{1,0:T(8,128)(2,1)S(1)}, bf16[3072,128]{1,0:T(8,128)(2,1)}, u32[]{:S(2)}, u32[]{:S(2)}) %collective-permute-start.1) | collective-permute-done | bytes 786464 | tf_op jit(solution)/shard_map/ppermute | solution.py:14
  128.3 55.1 %while.10 = (s32[]{:T(128)}, bf16[6,512,1,128]{3,1,2,0:T(8,128)(2,1)}, bf16[6,512,1,128]{3,1,2,0:T(8,128)(2,1)S(1)}, bf16[3072,1,128]{2,0,1:T(8,128)(2,1)S(1)}, ...) while((s32[]{:T(128)}, ...), condition=%wide.region_7.8_spmd, body=%wide.region_2.7_spmd.sunk | while | flops 1640692736 | bytes 41841764 | solution.py:83
  128.3 1.1 fusion.64
  129.4 1.1 multiply_reduce_fusion.2
  130.5 2.6 %fusion.66 = (f32[512]{0:T(512)S(1)}, f32[512]{0:T(512)S(1)}) fusion(f32[512,3072]{1,0:T(8,128)S(1)} %get-tuple-element.170, f32[512]{0:T(512)S(1)} %max.9, pred[]{:T(512)} %get-tuple-element.195, f32[512,3072]{1,0:T(8,128)S(1)} %get-tuple-element.167), kind=kLoop, calls=%fused_computation.7.clone.1 | loop fusion | flops 11009024 | bytes 12589057 | tf_op jit(solution)/shard_map/while/body/eval_jaxpr/reduce_sum | solution.py:34
  133.1 1.1 fusion.65
  134.3 3.2 %fusion.67 = bf16[6,512,1,128]{3,1,2,0:T(8,128)(2,1)} fusion(bf16[6,512,1,128]{3,1,2,0:T(8,128)(2,1)} %get-tuple-element.183, s32[]{:T(128)} %get-tuple-element.182, f32[512,128]{1,0:T(8,128)S(1)} %fusion.65, f32[512,3072]{1,0:T(8,128)S(1)} %get-tuple-element.170, f32[512]{0:T(512)S(1)} %max.9, pred[]{:T(512)} %get-tuple-element.195, ...), kind=kOutput, calls=%fused_computation.19.clone.1 | convolution fusion | flops 409141248 | bytes 7476224 | tf_op jit(solution)/shard_map/while/body/eval_jaxpr/hqk,khd->qhd/dot_general | solution.py:41
  137.5 1.1 fusion.64
  138.6 1.1 multiply_reduce_fusion.2
  139.7 2.6 %fusion.66 = (f32[512]{0:T(512)S(1)}, f32[512]{0:T(512)S(1)}) fusion(f32[512,3072]{1,0:T(8,128)S(1)} %get-tuple-element.170, f32[512]{0:T(512)S(1)} %max.9, pred[]{:T(512)} %get-tuple-element.195, f32[512,3072]{1,0:T(8,128)S(1)} %get-tuple-element.167), kind=kLoop, calls=%fused_computation.7.clone.1 | loop fusion | flops 11009024 | bytes 12589057 | tf_op jit(solution)/shard_map/while/body/eval_jaxpr/reduce_sum | solution.py:34
  142.3 1.1 fusion.65
  143.5 3.2 %fusion.67 = bf16[6,512,1,128]{3,1,2,0:T(8,128)(2,1)} fusion(bf16[6,512,1,128]{3,1,2,0:T(8,128)(2,1)} %get-tuple-element.183, s32[]{:T(128)} %get-tuple-element.182, f32[512,128]{1,0:T(8,128)S(1)} %fusion.65, f32[512,3072]{1,0:T(8,128)S(1)} %get-tuple-element.170, f32[512]{0:T(512)S(1)} %max.9, pred[]{:T(512)} %get-tuple-element.195, ...), kind=kOutput, calls=%fused_computation.19.clone.1 | convolution fusion | flops 409141248 | bytes 7476224 | tf_op jit(solution)/shard_map/while/body/eval_jaxpr/hqk,khd->qhd/dot_general | solution.py:41
  146.7 1.1 fusion.64
  147.8 1.1 multiply_reduce_fusion.2
  148.9 2.6 %fusion.66 = (f32[512]{0:T(512)S(1)}, f32[512]{0:T(512)S(1)}) fusion(f32[512,3072]{1,0:T(8,128)S(1)} %get-tuple-element.170, f32[512]{0:T(512)S(1)} %max.9, pred[]{:T(512)} %get-tuple-element.195, f32[512,3072]{1,0:T(8,128)S(1)} %get-tuple-element.167), kind=kLoop, calls=%fused_computation.7.clone.1 | loop fusion | flops 11009024 | bytes 12589057 | tf_op jit(solution)/shard_map/while/body/eval_jaxpr/reduce_sum | solution.py:34
  151.5 1.1 fusion.65
  152.6 3.2 %fusion.67 = bf16[6,512,1,128]{3,1,2,0:T(8,128)(2,1)} fusion(bf16[6,512,1,128]{3,1,2,0:T(8,128)(2,1)} %get-tuple-element.183, s32[]{:T(128)} %get-tuple-element.182, f32[512,128]{1,0:T(8,128)S(1)} %fusion.65, f32[512,3072]{1,0:T(8,128)S(1)} %get-tuple-element.170, f32[512]{0:T(512)S(1)} %max.9, pred[]{:T(512)} %get-tuple-element.195, ...), kind=kOutput, calls=%fused_computation.19.clone.1 | convolution fusion | flops 409141248 | bytes 7476224 | tf_op jit(solution)/shard_map/while/body/eval_jaxpr/hqk,khd->qhd/dot_general | solution.py:41
  155.9 1.1 fusion.64
  157.0 1.1 multiply_reduce_fusion.2
  158.1 2.6 %fusion.66 = (f32[512]{0:T(512)S(1)}, f32[512]{0:T(512)S(1)}) fusion(f32[512,3072]{1,0:T(8,128)S(1)} %get-tuple-element.170, f32[512]{0:T(512)S(1)} %max.9, pred[]{:T(512)} %get-tuple-element.195, f32[512,3072]{1,0:T(8,128)S(1)} %get-tuple-element.167), kind=kLoop, calls=%fused_computation.7.clone.1 | loop fusion | flops 11009024 | bytes 12589057 | tf_op jit(solution)/shard_map/while/body/eval_jaxpr/reduce_sum | solution.py:34
  160.7 1.1 fusion.65
  161.8 3.2 %fusion.67 = bf16[6,512,1,128]{3,1,2,0:T(8,128)(2,1)} fusion(bf16[6,512,1,128]{3,1,2,0:T(8,128)(2,1)} %get-tuple-element.183, s32[]{:T(128)} %get-tuple-element.182, f32[512,128]{1,0:T(8,128)S(1)} %fusion.65, f32[512,3072]{1,0:T(8,128)S(1)} %get-tuple-element.170, f32[512]{0:T(512)S(1)} %max.9, pred[]{:T(512)} %get-tuple-element.195, ...), kind=kOutput, calls=%fused_computation.19.clone.1 | convolution fusion | flops 409141248 | bytes 7476224 | tf_op jit(solution)/shard_map/while/body/eval_jaxpr/hqk,khd->qhd/dot_general | solution.py:41
  165.1 1.1 fusion.64
  166.2 1.1 multiply_reduce_fusion.2
  167.3 2.6 %fusion.66 = (f32[512]{0:T(512)S(1)}, f32[512]{0:T(512)S(1)}) fusion(f32[512,3072]{1,0:T(8,128)S(1)} %get-tuple-element.170, f32[512]{0:T(512)S(1)} %max.9, pred[]{:T(512)} %get-tuple-element.195, f32[512,3072]{1,0:T(8,128)S(1)} %get-tuple-element.167), kind=kLoop, calls=%fused_computation.7.clone.1 | loop fusion | flops 11009024 | bytes 12589057 | tf_op jit(solution)/shard_map/while/body/eval_jaxpr/reduce_sum | solution.py:34
  169.9 1.1 fusion.65
  171.0 3.2 %fusion.67 = bf16[6,512,1,128]{3,1,2,0:T(8,128)(2,1)} fusion(bf16[6,512,1,128]{3,1,2,0:T(8,128)(2,1)} %get-tuple-element.183, s32[]{:T(128)} %get-tuple-element.182, f32[512,128]{1,0:T(8,128)S(1)} %fusion.65, f32[512,3072]{1,0:T(8,128)S(1)} %get-tuple-element.170, f32[512]{0:T(512)S(1)} %max.9, pred[]{:T(512)} %get-tuple-element.195, ...), kind=kOutput, calls=%fused_computation.19.clone.1 | convolution fusion | flops 409141248 | bytes 7476224 | tf_op jit(solution)/shard_map/while/body/eval_jaxpr/hqk,khd->qhd/dot_general | solution.py:41
  174.2 1.1 fusion.64
  175.4 1.1 multiply_reduce_fusion.2
  176.4 2.6 %fusion.66 = (f32[512]{0:T(512)S(1)}, f32[512]{0:T(512)S(1)}) fusion(f32[512,3072]{1,0:T(8,128)S(1)} %get-tuple-element.170, f32[512]{0:T(512)S(1)} %max.9, pred[]{:T(512)} %get-tuple-element.195, f32[512,3072]{1,0:T(8,128)S(1)} %get-tuple-element.167), kind=kLoop, calls=%fused_computation.7.clone.1 | loop fusion | flops 11009024 | bytes 12589057 | tf_op jit(solution)/shard_map/while/body/eval_jaxpr/reduce_sum | solution.py:34
  179.1 1.1 fusion.65
  180.2 3.2 %fusion.67 = bf16[6,512,1,128]{3,1,2,0:T(8,128)(2,1)} fusion(bf16[6,512,1,128]{3,1,2,0:T(8,128)(2,1)} %get-tuple-element.183, s32[]{:T(128)} %get-tuple-element.182, f32[512,128]{1,0:T(8,128)S(1)} %fusion.65, f32[512,3072]{1,0:T(8,128)S(1)} %get-tuple-element.170, f32[512]{0:T(512)S(1)} %max.9, pred[]{:T(512)} %get-tuple-element.195, ...), kind=kOutput, calls=%fused_computation.19.clone.1 | convolution fusion | flops 409141248 | bytes 7476224 | tf_op jit(solution)/shard_map/while/body/eval_jaxpr/hqk,khd->qhd/dot_general | solution.py:41
  183.4 27.0 %all_to_all.64 = bf16[32,96,128]{2,1,0:T(8,128)(2,1)S(1)} all-to-all(bf16[32,96,128]{2,1,0:T(8,128)(2,1)} %bitcast.22), channel_id=1, replica_groups=mesh['section'=8,'seq'=32] {'seq'}, dimensions={0} | all-to-all | bytes 1572864 | tf_op jit(solution)/shard_map/all_to_all | solution.py:85
  210.7 1.2 broadcast_in_dim.21
  (28 shorter events, 2.9 us)
Async XLA Ops:
  0.0 16.0 %copy-start.1 = (bf16[1,96,4096]{2,1,0:T(8,128)(2,1)S(1)}, bf16[1,96,4096]{2,1,0:T(8,128)(2,1)}, u32[]{:S(2)}) copy-start(bf16[1,96,4096]{2,1,0:T(8,128)(2,1)} %param.8) | copy-start | bytes 2359300
  3.6 40.3 %copy-start = (bf16[1,96,4096]{2,1,0:T(8,128)(2,1)S(1)}, bf16[1,96,4096]{2,1,0:T(8,128)(2,1)}, u32[]{:S(2)}) copy-start(bf16[1,96,4096]{2,1,0:T(8,128)(2,1)} %param.6) | copy-start | bytes 2359300
  5.4 33.9 %all-to-all-start.1 = ((bf16[96,32,128]{2,0,1:T(8,128)(2,1)}), bf16[96,32,128]{2,0,1:T(8,128)(2,1)S(1)}, u32[]{:S(2)}, u32[]{:S(2)}) async-start(bf16[96,32,128]{2,0,1:T(8,128)(2,1)} %copy.28), calls=%async_computation.1 | async-start | bytes 1572864 | tf_op jit(solution)/shard_map/all_to_all | solution.py:56
  39.3 23.6 %all-to-all-start.2 = ((bf16[96,32,128]{2,0,1:T(8,128)(2,1)}), bf16[96,32,128]{2,0,1:T(8,128)(2,1)S(1)}, u32[]{:S(2)}, u32[]{:S(2)}) async-start(bf16[96,32,128]{2,0,1:T(8,128)(2,1)} %copy.29), calls=%async_computation.2 | async-start | bytes 1572864 | tf_op jit(solution)/shard_map/all_to_all | solution.py:57
  62.9 28.3 %all-to-all-start = ((bf16[96,32,128]{2,0,1:T(8,128)(2,1)}), bf16[96,32,128]{2,0,1:T(8,128)(2,1)S(1)}, u32[]{:S(2)}, u32[]{:S(2)}) async-start(bf16[96,32,128]{2,0,1:T(8,128)(2,1)} %copy.27), calls=%async_computation | async-start | bytes 1572864 | tf_op jit(solution)/shard_map/all_to_all | solution.py:55
  72.2 39.5 %collective-permute-start = (bf16[3072,128]{1,0:T(8,128)(2,1)S(1)}, bf16[3072,128]{1,0:T(8,128)(2,1)S(1)}, u32[]{:S(2)}, u32[]{:S(2)}) collective-permute-start(bf16[3072,128]{1,0:T(8,128)(2,1)S(1)} %bitcast.101), channel_id=1, source_target_pairs={{0,32},{32,64},{64,96},{96,128},{128,160},{160,192},{192,224},{1,3... | collective-permute-start | bytes 2359304 | tf_op jit(solution)/shard_map/ppermute | solution.py:14
  75.6 52.7 %collective-permute-start.1 = (bf16[3072,128]{1,0:T(8,128)(2,1)S(1)}, bf16[3072,128]{1,0:T(8,128)(2,1)}, u32[]{:S(2)}, u32[]{:S(2)}) collective-permute-start(bf16[3072,128]{1,0:T(8,128)(2,1)S(1)} %bitcast.103), channel_id=1, source_target_pairs={{0,32},{32,64},{64,96},{96,128},{128,160},{160,192},{192,224},{1,3... | collective-permute-start | bytes 2359304 | tf_op jit(solution)/shard_map/ppermute | solution.py:14
where the time goes:
time: 214 us; the launch traced here: 212 us
  waiting for transfers between devices  88.1 us (41%)
  matrix products  39.2 us (18%)
  starting transfers between devices  31.2 us (15%)
  blocking collectives  27 us (13%)
  other arithmetic  19.4 us (9%)
  local copies, waits for them, and re-layouts  6.69 us (3%)
    ppermute x2, waiting for transfers between devices, passed_along(): return lax.ppermute(block, axis, route)  37.1 us
    all_to_all x1, blocking collectives, local(): lax.all_to_all(attended, 'seq', split_axis=0, concat_axis=1, tiled=True)  27 us
    all_to_all x1, waiting for transfers between devices, local(): lax.all_to_all(key_norm, 'seq', split_axis=1, concat_axis=0, tiled=True)  22 us
    dot_general x6, matrix products, finish(): jnp.einsum('hqk,khd->qhd', prior_expo.astype(jnp.bfloat16), prior_values,...  19.3 us
    all_to_all x1, waiting for transfers between devices, local(): lax.all_to_all(value_rows, 'seq', split_axis=1, concat_axis=0, tiled=True)  16.9 us
    reduce_sum x6, other arithmetic, finish(): jnp.sum(prior_expo, axis=2, keepdims=True)  15.7 us
    dot_general x12, matrix products, block_scores(): jnp.einsum('qhd,khd->hqk', query_block, key_rows, preferred_element_type=...  13.2 us
    all_to_all x1, waiting for transfers between devices, local(): lax.all_to_all(query_norm, 'seq', split_axis=1, concat_axis=0, tiled=True)  12.2 us
  transfers between devices with their start and end apart: 5, of which 5 were waited for; matrix products, arithmetic and copies ran while one was open for 2% of the time, Pallas kernels for 0%

commit v1 on v0

v1 whole, which is shorter than its diff:
```python
import math

import jax
import jax.numpy as jnp
from jax import lax
from jax.experimental import pallas as pl
from jax.experimental.pallas import tpu as pltpu
from jax.sharding import PartitionSpec as P

HEAD_DIM = 128
EXPONENT_SCALE = math.log2(math.e) / math.sqrt(HEAD_DIM)
F32 = jnp.float32
BF16 = jnp.bfloat16
VMEM_LIMIT = 60 * 2**20
LAST_WITH_LAST = (((1,), (1,)), ((), ()))


def norm_rows(rows, gain):
    wide = rows.astype(F32)
    power = jnp.mean(wide * wide, axis=-1, keepdims=True)
    return (wide * lax.rsqrt(power + 1e-06) * gain).astype(BF16)


def split_heads(rows, chips, width):
    return [rows[:, c * width : (c + 1) * width] for c in range(chips)]


def prepare_keys_values(keys, values, gains, chips, heads):
    tokens, features = keys.shape

    def kernel(key_ref, value_ref, gain_ref, *out_refs):
        normed = norm_rows(key_ref[...], gain_ref[1:2, :])
        for h in range(heads):
            for c in range(chips):
                lo = (c * heads + h) * HEAD_DIM
                out_refs[h][c, 0] = normed[:, lo : lo + HEAD_DIM]
                out_refs[h][c, 1] = value_ref[:, lo : lo + HEAD_DIM]

    vmem = pl.BlockSpec(memory_space=pltpu.VMEM)
    return pl.pallas_call(
        kernel,
        in_specs=[vmem] * 3,
        out_specs=[vmem] * heads,
        out_shape=[jax.ShapeDtypeStruct((chips, 2, tokens, HEAD_DIM), BF16)] * heads,
        compiler_params=pltpu.CompilerParams(vmem_limit_bytes=VMEM_LIMIT),
        name="prepare_kv",
    )(keys, values, gains)


def prepare_queries(queries, gains, chips, heads):
    tokens, features = queries.shape

    def kernel(query_ref, gain_ref, out_ref):
        normed = norm_rows(query_ref[...], gain_ref[0:1, :])
        for c in range(chips):
            for h in range(heads):
                lo = (c * heads + h) * HEAD_DIM
                out_ref[c, h] = normed[:, lo : lo + HEAD_DIM]

    vmem = pl.BlockSpec(memory_space=pltpu.VMEM)
    return pl.pallas_call(
        kernel,
        in_specs=[vmem] * 2,
        out_specs=vmem,
        out_shape=jax.ShapeDtypeStruct((chips, heads, tokens, HEAD_DIM), BF16),
        compiler_params=pltpu.CompilerParams(vmem_limit_bytes=VMEM_LIMIT),
        name="prepare_q",
    )(queries, gains)


def attend(has_prior, queries, head, pieces, earlier_out, rows_block=256, keys_block=512):
    chips, heads, tokens, _ = queries.shape
    length = chips * tokens
    blocks = length // rows_block
    keys_each = length
    per = keys_each // keys_block
    cost = pl.CostEstimate(
        flops=4 * length * 4 * keys_each * HEAD_DIM,
        bytes_accessed=2 * 10 * length * HEAD_DIM,
        transcendentals=4 * length * keys_each,
    )

    def kernel(prior_ref, query_ref, *refs):
        kv = refs[:4]
        out_ref = refs[-7]
        query_rows, out_rows, scores_a, scores_b, top_a, top_b = refs[-6:]

        def piece(c, which):
            b, t = divmod(c, per)
            rows = kv[b][:, which].reshape(keys_each, HEAD_DIM)
            return rows[t * keys_block : (t + 1) * keys_block]

        def phase(ahead, behind, count):
            if ahead:
                ahead_scores, ahead_top, block = ahead
                query = query_rows[pl.ds(block * rows_block, rows_block), :]
                top = None
            if behind:
                behind_scores, behind_top, block_out = behind
                shift = jnp.max(behind_top[...], axis=1, keepdims=True) * EXPONENT_SCALE
                shift = jnp.broadcast_to(shift, (rows_block, HEAD_DIM))
                total = None
                mixed = None
            for c in range(count):
                base = c * keys_block
                if ahead:
                    raw = lax.dot_general(
                        query, piece(c, 0), LAST_WITH_LAST, preferred_element_type=F32
                    )
                    ahead_scores[:, base : base + keys_block] = raw
                    for j in range(0, keys_block, 128):
                        part = raw[:, j : j + 128]
                        top = part if top is None else jnp.maximum(top, part)
                if behind:
                    weights = []
                    for j in range(base, base + keys_block, 128):
                        expo = jnp.exp2(behind_scores[:, j : j + 128] * EXPONENT_SCALE - shift)
                        total = expo if total is None else total + expo
                        weights.append(expo.astype(BF16))
                    part = jnp.dot(
                        jnp.concatenate(weights, axis=1),
                        piece(c, 1),
                        preferred_element_type=F32,
                    )
                    mixed = part if mixed is None else mixed + part
            if ahead:
                ahead_top[...] = top
            if behind:
                total = jnp.sum(total, axis=1, keepdims=True)
                out_rows[pl.ds(block_out * rows_block, rows_block), :] = (mixed / total).astype(BF16)

        def whole(count):
            a, b = (scores_a, top_a), (scores_b, top_b)
            phase(a + (0,), None, count)

            def pair(i, carry):
                phase(b + (2 * i + 1,), a + (2 * i,), count)
                phase(a + (2 * i + 2,), b + (2 * i + 1,), count)
                return carry

            lax.fori_loop(0, blocks // 2 - 1, pair, 0)
            phase(b + (blocks - 1,), a + (blocks - 2,), count)
            phase(None, b + (blocks - 1,), count)

        query_rows[...] = query_ref[:, 0].reshape(length, HEAD_DIM)

        @pl.when(prior_ref[0] > 0)
        def _():
            whole(4 * per)

        @pl.when(prior_ref[0] == 0)
        def _():
            whole(2 * per)

        out_ref[:, 0] = out_rows[...].reshape(chips, tokens, HEAD_DIM)

    one_head = pl.BlockSpec((chips, 1, tokens, HEAD_DIM), lambda i: (0, head, 0, 0))
    kv_spec = pl.BlockSpec((chips, 2, tokens, HEAD_DIM), lambda i: (0, 0, 0, 0))
    in_specs = [pl.BlockSpec(memory_space=pltpu.SMEM), one_head] + [kv_spec] * 4
    operands = [has_prior, queries, *pieces]
    aliases = {}
    if earlier_out is not None:
        in_specs.append(pl.BlockSpec(memory_space=pl.ANY))
        aliases = {len(operands): 0}
        operands.append(earlier_out)
    return pl.pallas_call(
        kernel,
        grid=(1,),
        in_specs=in_specs,
        out_specs=one_head,
        out_shape=jax.ShapeDtypeStruct(queries.shape, BF16),
        scratch_shapes=[
            pltpu.VMEM((length, HEAD_DIM), BF16),
            pltpu.VMEM((length, HEAD_DIM), BF16),
            pltpu.VMEM((rows_block, 4 * keys_each), F32),
            pltpu.VMEM((rows_block, 4 * keys_each), F32),
            pltpu.VMEM((rows_block, HEAD_DIM), F32),
            pltpu.VMEM((rows_block, HEAD_DIM), F32),
        ],
        input_output_aliases=aliases,
        cost_estimate=cost,
        compiler_params=pltpu.CompilerParams(vmem_limit_bytes=VMEM_LIMIT),
        name="attend",
    )(*operands)


def local(queries, keys, values, norm_gains):
    seq = lax.axis_size("seq")
    sections = lax.axis_size("section")
    chips = seq // 2
    tokens, features = queries.shape[1:]
    heads = features // HEAD_DIM // chips
    same_core = [[2 * p + c for p in range(chips)] for c in range(2)]

    def exchange(x):
        return lax.all_to_all(
            x, "seq", split_axis=0, concat_axis=0, tiled=True, axis_index_groups=same_core
        )

    def swap(x):
        return lax.ppermute(x, "seq", [(i, i ^ 1) for i in range(seq)])

    def passed_on(x):
        return lax.ppermute(x, "section", [(s, s + 1) for s in range(sections - 1)])

    has_prior = (lax.axis_index("section") > 0).astype(jnp.int32).reshape(1)
    sent = prepare_keys_values(keys[0], values[0], norm_gains, chips, heads)
    both = exchange(jnp.concatenate(sent, axis=1))
    own = [both[:, 2 * h : 2 * h + 2] for h in range(heads)]
    query_sent = prepare_queries(queries[0], norm_gains, chips, heads)
    query_sent, own = lax.optimization_barrier((query_sent, own))
    prior = [passed_on(x) for x in own]
    head_queries = exchange(query_sent)
    own_other = [swap(x) for x in own]
    prior_other = [swap(x) for x in prior]
    out = None
    for h in range(heads):
        pieces = (own[h], own_other[h], prior[h], prior_other[h])
        out = attend(has_prior, head_queries, h, pieces, out)
    back = exchange(out)
    return jnp.transpose(back, (2, 0, 1, 3)).reshape(1, tokens, features)


def solution(mesh):
    return jax.shard_map(
        local,
        mesh=mesh,
        in_specs=(
            P("section", "seq", None),
            P("section", "seq", None),
            P("section", "seq", None),
            P(),
        ),
        out_specs=P("section", "seq", None),
        check_vma=False,
    )
```

time: 214 us -> 177 us (0.83)
  Pallas kernels: 0 us -> 40.6 us
  matrix products: 39.2 us -> 0 us
  other arithmetic: 19.4 us -> 2.67 us
  starting transfers between devices: 31.2 us -> 22.2 us
  waiting for transfers between devices: 88.1 us -> 82.7 us
  local copies, waits for them, and re-layouts: 6.69 us -> 3.13 us
    pallas_call x0 -> x4, Pallas kernels: none -> 40.6 us  [the longest x2 35.1 us: attend(): pl.pallas_call(kernel, grid=(1,), in_specs=in_specs, out_specs=one_head,...]
    dot_general x24 -> x0, matrix products: 39.2 us -> none  [the longest x6 19.3 us: finish(): jnp.einsum('hqk,khd->qhd', prior_expo.astype(jnp.bfloat16), prior_values,...]
    reduce_sum x8 -> x0, other arithmetic: 17.4 us -> none  [the longest x6 15.7 us: finish(): jnp.sum(prior_expo, axis=2, keepdims=True)]
    all_to_all x3 -> x2, waiting for transfers between devices: 51.1 us -> 38 us  [exchange(): lax.all_to_all(x, 'seq', split_axis=0, concat_axis=0, tiled=True, axis_in...]
    all_to_all x3 -> x2, starting transfers between devices: 24.4 us -> 14.8 us  [exchange(): lax.all_to_all(x, 'seq', split_axis=0, concat_axis=0, tiled=True, axis_in...]
    ppermute x2 -> x6, waiting for transfers between devices: 37.1 us -> 44.7 us  [the longest x2 44.7 us: passed_on(): return lax.ppermute(x, 'section', [(s, s + 1) for s in range(sections - 1)])]
    concatenate x0 -> x1, other arithmetic: none -> 2.67 us  [local(): both = exchange(jnp.concatenate(sent, axis=1))]
    convert_element_type x2 -> x0, local copies, waits for them, and re-layouts: 2.4 us -> none  [normalize(): return (wide * lax.rsqrt(power + 1e-06) * gain).astype(jnp.bfloat16)]
  transfers between devices with their start and end apart: 5 -> 8, of which waited for: 5 -> 3; matrix products, arithmetic and copies ran while one was open for 2% -> 0% of each run, Pallas kernels for 0% -> 11%
where the time goes in v1:
time: 177 us
  waiting for transfers between devices  82.7 us (47%)
  Pallas kernels  40.6 us (23%)
  blocking collectives  25.2 us (14%)
  starting transfers between devices  22.2 us (13%)
  local copies, waits for them, and re-layouts  3.13 us (2%)
  other arithmetic  2.67 us (2%)
    ppermute x2, waiting for transfers between devices, passed_on(): return lax.ppermute(x, 'section', [(s, s + 1) for s in range(sections - 1)])  44.7 us
    all_to_all x2, waiting for transfers between devices, exchange(): lax.all_to_all(x, 'seq', split_axis=0, concat_axis=0, tiled=True, axis_in...  38 us
    pallas_call x2, Pallas kernels, attend(): pl.pallas_call(kernel, grid=(1,), in_specs=in_specs, out_specs=one_head,...  35.1 us
    all_to_all x1, blocking collectives, exchange(): lax.all_to_all(x, 'seq', split_axis=0, concat_axis=0, tiled=True, axis_in...  25.2 us
    all_to_all x2, starting transfers between devices, exchange(): lax.all_to_all(x, 'seq', split_axis=0, concat_axis=0, tiled=True, axis_in...  14.8 us
    ppermute x2, starting transfers between devices, passed_on(): return lax.ppermute(x, 'section', [(s, s + 1) for s in range(sections - 1)])  6.8 us
  transfers between devices with their start and end apart: 8, of which 3 were waited for; matrix products, arithmetic and copies ran while one was open for 0% of the time, Pallas kernels for 11%

profile of v1, /device:TPU:32, one launch (start us, length us, event | category | flops | bytes accessed | tf_op | source)
XLA Modules:
  0.0 176.7 jit_solution(5172133462013771839)
XLA Ops:
  0.0 3.0 %prepare_kv.1 = (bf16[16,2,96,128]{3,2,1,0:T(8,128)(2,1)}, bf16[16,2,96,128]{3,2,1,0:T(8,128)(2,1)}) custom-call(bf16[96,4096]{1,0:T(8,128)(2,1)} %bitcast.6, bf16[96,4096]{1,0:T(8,128)(2,1)} %bitcast.7, f32[2,4096]{1,0:T(2,128)} %gain_ref.3), custom_call_target="tpu_custom_call" | custom-call | tf_op jit(solution)/shard_map/prepare_kv/pallas_call | solution.py:40
  3.0 2.7 %pad_maximum_fusion = bf16[16,4,96,128]{3,2,1,0:T(8,128)(2,1)} fusion(bf16[16,2,96,128]{3,2,1,0:T(8,128)(2,1)} %get-tuple-element.11, bf16[16,2,96,128]{3,2,1,0:T(8,128)(2,1)} %get-tuple-element.10), kind=kLoop, calls=%fused_computation | loop fusion | flops 786432 | bytes 3145728 | tf_op jit(solution)/shard_map/concatenate | solution.py:208
  5.7 10.3 %all-to-all-start = ((bf16[16,4,96,128]{3,2,1,0:T(8,128)(2,1)}), bf16[16,4,96,128]{3,2,1,0:T(8,128)(2,1)S(1)}, u32[]{:S(2)}, u32[]{:S(2)}) async-start(bf16[16,4,96,128]{3,2,1,0:T(8,128)(2,1)} %pad_maximum_fusion), calls=%async_computation | async-start | bytes 3145728 | tf_op jit(solution)/shard_map/all_to_all | solution.py:196
  16.0 2.5 %prepare_q.1 = bf16[16,2,96,128]{3,2,1,0:T(8,128)(2,1)} custom-call(bf16[96,4096]{1,0:T(8,128)(2,1)} %bitcast.8, f32[2,4096]{1,0:T(2,128)} %gain_ref.3), custom_call_target="tpu_custom_call" | custom-call | tf_op jit(solution)/shard_map/prepare_q/pallas_call | solution.py:61
  18.5 38.0 %all-to-all-done = bf16[16,4,96,128]{3,2,1,0:T(8,128)(2,1)S(1)} async-done(((bf16[16,4,96,128]{3,2,1,0:T(8,128)(2,1)}), bf16[16,4,96,128]{3,2,1,0:T(8,128)(2,1)S(1)}, u32[]{:S(2)}, u32[]{:S(2)}) %all-to-all-start) | async-done | bytes 1572896 | tf_op jit(solution)/shard_map/all_to_all | solution.py:196
  56.5 0.1 fusion
  56.6 0.0 copy-start.2
  56.6 0.0 copy-start.1
  56.6 3.4 %collective-permute-start.4 = (bf16[16,2,96,128]{3,2,1,0:T(8,128)(2,1)S(1)}, bf16[16,2,96,128]{3,2,1,0:T(8,128)(2,1)}, u32[]{:S(2)}, u32[]{:S(2)}) collective-permute-start(bf16[16,2,96,128]{3,2,1,0:T(8,128)(2,1)S(1)} %get-tuple-element.14.refs_0_), channel_id=1, source_target_pairs={{0,32},{32,64},{64,96},{96,128},{128,160},{160,192},{192,224},{1,3... | collective-permute-start | bytes 2359304 | tf_op jit(solution)/shard_map/ppermute | solution.py:204
  60.0 4.5 %all-to-all-start.1 = ((bf16[16,2,96,128]{3,2,1,0:T(8,128)(2,1)}), bf16[16,2,96,128]{3,2,1,0:T(8,128)(2,1)S(1)}, u32[]{:S(2)}, u32[]{:S(2)}) async-start(bf16[16,2,96,128]{3,2,1,0:T(8,128)(2,1)} %prepare_q.1), calls=%async_computation.1 | async-start | bytes 1572864 | tf_op jit(solution)/shard_map/all_to_all | solution.py:196
  64.6 3.4 %collective-permute-start.1 = (bf16[16,2,96,128]{3,2,1,0:T(8,128)(2,1)S(1)}, bf16[16,2,96,128]{3,2,1,0:T(8,128)(2,1)S(1)}, u32[]{:S(2)}, u32[]{:S(2)}) collective-permute-start(bf16[16,2,96,128]{3,2,1,0:T(8,128)(2,1)S(1)} %get-tuple-element.13.refs_0_), channel_id=1, source_target_pairs={{0,32},{32,64},{64,96},{96,128},{128,160},{160,192},{192,224},{1,3... | collective-permute-start | bytes 2359304 | tf_op jit(solution)/shard_map/ppermute | solution.py:204
  68.0 0.1 collective-permute-start.3
  68.1 17.3 %collective-permute-done.4.refs_2_ = bf16[16,2,96,128]{3,2,1,0:T(8,128)(2,1)} collective-permute-done((bf16[16,2,96,128]{3,2,1,0:T(8,128)(2,1)S(1)}, bf16[16,2,96,128]{3,2,1,0:T(8,128)(2,1)}, u32[]{:S(2)}, u32[]{:S(2)}) %collective-permute-start.4) | collective-permute-done | bytes 786464 | tf_op jit(solution)/shard_map/ppermute | solution.py:204
  85.4 0.0 collective-permute-start.5
  85.4 0.5 collective-permute-start
  85.9 27.4 %collective-permute-done.1.refs_2_ = bf16[16,2,96,128]{3,2,1,0:T(8,128)(2,1)S(1)} collective-permute-done((bf16[16,2,96,128]{3,2,1,0:T(8,128)(2,1)S(1)}, bf16[16,2,96,128]{3,2,1,0:T(8,128)(2,1)S(1)}, u32[]{:S(2)}, u32[]{:S(2)}) %collective-permute-start.1) | collective-permute-done | bytes 786464 | tf_op jit(solution)/shard_map/ppermute | solution.py:204
  113.3 0.0 copy-start.3
  113.3 0.0 collective-permute-start.2
  113.3 0.0 collective-permute-done.3.refs_1_
  113.3 0.0 all-to-all-done.1.query_ref
  113.3 0.0 copy-start
  113.3 0.0 collective-permute-done.5.refs_3_
  113.3 0.0 copy-done.2
  113.4 0.9 copy-done
  114.3 17.6 %attend.2.refs_4_ = bf16[16,2,96,128]{3,2,1,0:T(8,128)(2,1)} custom-call(s32[1]{0:T(128)} %bitcast.prior_ref, bf16[16,2,96,128]{3,2,1,0:T(8,128)(2,1)} %copy-done, bf16[16,2,96,128]{3,2,1,0:T(8,128)(2,1)} %copy-done.2, bf16[16,2,96,128]{3,2,1,0:T(8,128)(2,1)} %collective-permute-done.3.refs_1_, bf16[16,2,96,128]{3,2,1,0:T(8,128)(2,1)} %collective-permute-done.4.refs_2_, ...), custom_call_target="tpu_custom_call" | custom-call | flops 4831838208 | bytes 3932160 | tf_op jit(solution)/shard_map/attend/pallas_call | solution.py:166
  131.9 0.0 copy-done.1
  131.9 0.0 copy-done.3
  131.9 0.0 collective-permute-done.refs_1_
  131.9 0.0 collective-permute-done.2.refs_3_
  131.9 17.5 %attend.3 = bf16[16,2,96,128]{3,2,1,0:T(8,128)(2,1)} custom-call(s32[1]{0:T(128)} %bitcast.prior_ref, bf16[16,2,96,128]{3,2,1,0:T(8,128)(2,1)} %copy-done, bf16[16,2,96,128]{3,2,1,0:T(8,128)(2,1)} %copy-done.1, bf16[16,2,96,128]{3,2,1,0:T(8,128)(2,1)} %collective-permute-done.refs_1_, ...), custom_call_target="tpu_custom_call", output_to_operand_aliasing={{}: (6, {})} | custom-call | flops 4831838208 | bytes 3932160 | tf_op jit(solution)/shard_map/attend/pallas_call | solution.py:166
  149.4 25.2 %all_to_all.15 = bf16[16,2,96,128]{3,2,1,0:T(8,128)(2,1)S(1)} all-to-all(bf16[16,2,96,128]{3,2,1,0:T(8,128)(2,1)} %attend.3), channel_id=1, replica_groups={{0,2,4,6,8,10,12,14,16,18,20,22,24,26,28,30},{1,3,5,7,9,11,13,15,17,19,..., dimensions={0} | all-to-all | bytes 1572864 | tf_op jit(solution)/shard_map/all_to_all | solution.py:196
  174.6 0.6 copy.6
  175.2 1.5 reshape.10
Async XLA Ops:
  5.7 50.8 %all-to-all-start = ((bf16[16,4,96,128]{3,2,1,0:T(8,128)(2,1)}), bf16[16,4,96,128]{3,2,1,0:T(8,128)(2,1)S(1)}, u32[]{:S(2)}, u32[]{:S(2)}) async-start(bf16[16,4,96,128]{3,2,1,0:T(8,128)(2,1)} %pad_maximum_fusion), calls=%async_computation | async-start | bytes 3145728 | tf_op jit(solution)/shard_map/all_to_all | solution.py:196
  56.6 56.7 %copy-start.2 = (bf16[16,2,96,128]{3,2,1,0:T(8,128)(2,1)}, bf16[16,2,96,128]{3,2,1,0:T(8,128)(2,1)S(1)}, u32[]{:S(2)}) copy-start(bf16[16,2,96,128]{3,2,1,0:T(8,128)(2,1)S(1)} %get-tuple-element.14.refs_0_) | copy-start | bytes 2359300
  56.6 75.3 %copy-start.1 = (bf16[16,2,96,128]{3,2,1,0:T(8,128)(2,1)}, bf16[16,2,96,128]{3,2,1,0:T(8,128)(2,1)S(1)}, u32[]{:S(2)}) copy-start(bf16[16,2,96,128]{3,2,1,0:T(8,128)(2,1)S(1)} %get-tuple-element.13.refs_0_) | copy-start | bytes 2359300
  56.6 28.8 %collective-permute-start.4 = (bf16[16,2,96,128]{3,2,1,0:T(8,128)(2,1)S(1)}, bf16[16,2,96,128]{3,2,1,0:T(8,128)(2,1)}, u32[]{:S(2)}, u32[]{:S(2)}) collective-permute-start(bf16[16,2,96,128]{3,2,1,0:T(8,128)(2,1)S(1)} %get-tuple-element.14.refs_0_), channel_id=1, source_target_pairs={{0,32},{32,64},{64,96},{96,128},{128,160},{160,192},{192,224},{1,3... | collective-permute-start | bytes 2359304 | tf_op jit(solution)/shard_map/ppermute | solution.py:204
  60.0 53.3 %all-to-all-start.1 = ((bf16[16,2,96,128]{3,2,1,0:T(8,128)(2,1)}), bf16[16,2,96,128]{3,2,1,0:T(8,128)(2,1)S(1)}, u32[]{:S(2)}, u32[]{:S(2)}) async-start(bf16[16,2,96,128]{3,2,1,0:T(8,128)(2,1)} %prepare_q.1), calls=%async_computation.1 | async-start | bytes 1572864 | tf_op jit(solution)/shard_map/all_to_all | solution.py:196
  64.6 48.7 %collective-permute-start.1 = (bf16[16,2,96,128]{3,2,1,0:T(8,128)(2,1)S(1)}, bf16[16,2,96,128]{3,2,1,0:T(8,128)(2,1)S(1)}, u32[]{:S(2)}, u32[]{:S(2)}) collective-permute-start(bf16[16,2,96,128]{3,2,1,0:T(8,128)(2,1)S(1)} %get-tuple-element.13.refs_0_), channel_id=1, source_target_pairs={{0,32},{32,64},{64,96},{96,128},{128,160},{160,192},{192,224},{1,3... | collective-permute-start | bytes 2359304 | tf_op jit(solution)/shard_map/ppermute | solution.py:204
  68.0 45.3 %collective-permute-start.3 = (bf16[16,2,96,128]{3,2,1,0:T(8,128)(2,1)S(1)}, bf16[16,2,96,128]{3,2,1,0:T(8,128)(2,1)}, u32[]{:S(2)}, u32[]{:S(2)}) collective-permute-start(bf16[16,2,96,128]{3,2,1,0:T(8,128)(2,1)S(1)} %get-tuple-element.14.refs_0_), channel_id=1, source_target_pairs={{0,1},{1,0},{2,3},{3,2},{4,5},{5,4},{6,7},{7,6},{8,9},{9,8},{10,11... | collective-permute-start | bytes 2359304 | tf_op jit(solution)/shard_map/ppermute | solution.py:201
  85.4 27.9 %collective-permute-start.5 = (bf16[16,2,96,128]{3,2,1,0:T(8,128)(2,1)}, bf16[16,2,96,128]{3,2,1,0:T(8,128)(2,1)}, u32[]{:S(2)}, u32[]{:S(2)}) collective-permute-start(bf16[16,2,96,128]{3,2,1,0:T(8,128)(2,1)} %collective-permute-done.4.refs_2_), channel_id=1, source_target_pairs={{0,1},{1,0},{2,3},{3,2},{4,5},{5,4},{6,7},{7,6},{8,9},{9,8},{10,11... | collective-permute-start | bytes 2359304 | tf_op jit(solution)/shard_map/ppermute | solution.py:201
  85.4 46.5 %collective-permute-start = (bf16[16,2,96,128]{3,2,1,0:T(8,128)(2,1)S(1)}, bf16[16,2,96,128]{3,2,1,0:T(8,128)(2,1)}, u32[]{:S(2)}, u32[]{:S(2)}) collective-permute-start(bf16[16,2,96,128]{3,2,1,0:T(8,128)(2,1)S(1)} %get-tuple-element.13.refs_0_), channel_id=1, source_target_pairs={{0,1},{1,0},{2,3},{3,2},{4,5},{5,4},{6,7},{7,6},{8,9},{9,8},{10,11... | collective-permute-start | bytes 2359304 | tf_op jit(solution)/shard_map/ppermute | solution.py:201
  113.3 18.6 %copy-start.3 = (bf16[16,2,96,128]{3,2,1,0:T(8,128)(2,1)}, bf16[16,2,96,128]{3,2,1,0:T(8,128)(2,1)S(1)}, u32[]{:S(2)}) copy-start(bf16[16,2,96,128]{3,2,1,0:T(8,128)(2,1)S(1)} %collective-permute-done.1.refs_2_) | copy-start | bytes 2359300
  113.3 18.6 %collective-permute-start.2 = (bf16[16,2,96,128]{3,2,1,0:T(8,128)(2,1)S(1)}, bf16[16,2,96,128]{3,2,1,0:T(8,128)(2,1)}, u32[]{:S(2)}, u32[]{:S(2)}) collective-permute-start(bf16[16,2,96,128]{3,2,1,0:T(8,128)(2,1)S(1)} %collective-permute-done.1.refs_2_), channel_id=1, source_target_pairs={{0,1},{1,0},{2,3},{3,2},{4,5},{5,4},{6,7},{7,6},{8,9},{9,8},{10,11... | collective-permute-start | bytes 2359304 | tf_op jit(solution)/shard_map/ppermute | solution.py:201
  113.3 1.0 copy-start
